TPU v7x, 256 devices: a whole 4x4x8 slice. The times are simulated.
256 devices in a mesh: row: 64 (over z, y, x_hi), col: 2 (over core), layer: 2 (over x_lo).
Axes of the slice: x: 4 (x_hi: 2, x_lo: 2; x = x_hi * 2 + x_lo), y: 4, z: 8, core: 2. Of those that a mesh axis runs over, the one named last changes fastest.
Arguments:
- matrix: float32 [1, 64, 256, 32, 2, 256], P(None, 'row', None, None, 'col'), may hold values from -8 to 113.137085, as said below
Outputs:
- factored: float32 [1, 64, 256, 32, 2, 256], P(None, 'row', None, 'layer', 'col')
Inputs may be any that keep to these rules, and one draw needn't show every extreme that they name: `matrix`: viewed as in the first step it is symmetric, its leading 2 * 256 x 2 * 256 block is positive definite, and its diagonal entries lie between 2.5 and 5 times the square root of 512.
All inputs are finite; a program needn't handle non-finite values.
Results may differ from a plain program's by a relative error of at most 0.000059.
Values sent between devices are 32-bit elements; how exact they have to be, the bound alone decides.
A program may use at most 128 MiB of HBM per device.

v0:
```python
import jax
import jax.numpy as jnp
from jax import lax
from jax.sharding import PartitionSpec as P

HIGH = lax.Precision.HIGHEST


def from_root(shard, axis, root):
    mine = lax.axis_index(axis) == root
    return lax.psum(jnp.where(mine, shard, jnp.zeros_like(shard)), axis)


def factor_block(diag_block):
    lower_fac = jnp.linalg.cholesky(diag_block)
    identity = jnp.eye(diag_block.shape[0], dtype=jnp.float32)
    inverse = lax.linalg.triangular_solve(lower_fac, identity, left_side=True, lower=True)
    return (lower_fac, inverse)


def on_device(matrix):
    row_total = lax.axis_size("row")
    col_total = lax.axis_size("col")
    layer_total = lax.axis_size("layer")
    grid_row = lax.axis_index("row")
    grid_col = lax.axis_index("col")
    grid_layer = lax.axis_index("layer")
    row_blocks = matrix.shape[0]
    block_size = matrix.shape[2]
    col_blocks = matrix.shape[3]
    half = block_size // layer_total
    owned = col_blocks // layer_total
    rows = row_blocks * block_size
    tile = matrix.reshape(rows, col_blocks * block_size)
    row_ids = jnp.arange(rows) // block_size * row_total + grid_row
    column = tile[:, :block_size]
    base = tile
    pending = None
    total = None
    panels = []
    for section in range(2):
        first = section // row_total * block_size
        diag_block = from_root(column, "row", section % row_total)
        lower_fac, inverse = factor_block(diag_block)
        solved = jnp.dot(column, inverse.T, precision=HIGH, preferred_element_type=jnp.float32)
        repeated = jnp.tile(lower_fac, (row_blocks, 1))
        complete = jnp.where(
            row_ids[:, None] > section,
            solved,
            jnp.where(row_ids[:, None] == section, repeated, 0.0),
        )
        panels.append(complete)
        share = lax.dynamic_slice_in_dim(complete, grid_layer * half, half, 1)
        share = from_root(share, "col", section % col_total)
        gathered = lax.all_gather(
            share.reshape(row_blocks, 1, block_size, half), "row", axis=1, tiled=True
        )
        grouped = gathered.reshape(col_blocks, col_total, block_size, half)
        picked = lax.dynamic_index_in_dim(grouped, grid_col, 1, keepdims=False).reshape(
            col_blocks * block_size, half
        )
        update = lax.dot_general(
            share,
            picked,
            (((1,), (1,)), ((), ())),
            precision=HIGH,
            preferred_element_type=jnp.float32,
        )
        if section == 0:
            shares = lax.psum_scatter(
                update.reshape(rows, col_blocks, block_size),
                "layer",
                scatter_dimension=1,
                tiled=True,
            )
            summed = lax.all_gather(shares, "layer", axis=1, tiled=True)
            base = tile - summed.reshape(rows, col_blocks * block_size)
            column = base[:, :block_size]
        else:
            total = update
    reduced = lax.psum_scatter(
        total.reshape(rows, col_blocks, block_size), "layer", scatter_dimension=1, tiled=True
    )
    own_part = (
        lax.dynamic_slice_in_dim(
            base.reshape(rows, col_blocks, block_size), grid_layer * owned, owned, 1
        )
        - reduced
    )
    replacement = jnp.where(grid_col == 0, panels[0], panels[1])
    global_ids = (grid_layer * owned + jnp.arange(owned)) * col_total + grid_col
    result = jnp.where((global_ids < 2)[None, :, None], replacement[:, None, :], own_part)
    return result.reshape(row_blocks, 1, block_size, owned, 1, block_size)


def solution(mesh):
    in_specs = (P(None, "row", None, None, "col", None),)
    out_specs = P(None, "row", None, "layer", "col", None)
    return jax.shard_map(
        on_device, mesh=mesh, in_specs=in_specs, out_specs=out_specs, check_vma=False
    )
```

profile of v0, /device:TPU:6, one launch (start us, length us, event | category | flops | bytes accessed | tf_op | source)
XLA Modules:
  0.0 2254.5 jit_solution(14971382910372576024)
XLA Ops:
  6.5 19.4 copy.22
  27.8 642.9 %all-reduce.6.cloned.1.call-done = f32[256,256]{0,1:T(8,128)} async-done(((f32[256,256]{0,1:T(8,128)}), f32[256,256]{0,1:T(8,128)}) %all-reduce.6.cloned.1.call-update) | async-done | bytes 262160 | tf_op jit(solution)/shard_map/psum | solution.py:11
  672.8 11.7 cholesky.130
  684.5 9.8 custom-call.13
  694.8 11.7 cholesky.147
  708.9 4.3 while.4
  713.2 19.7 custom-call.14
  735.9 27.1 %all-reduce.8.cloned.1.call-done = f32[256,128]{0,1:T(8,128)} async-done(((f32[256,128]{0,1:T(8,128)}), f32[256,128]{0,1:T(8,128)}) %all-reduce.8.cloned.1.call-update) | async-done | bytes 131088 | tf_op jit(solution)/shard_map/psum | solution.py:11
  763.1 162.0 %all-gather.8.cloned.1.call-done = f32[16384,128]{0,1:T(8,128)} async-done(((f32[256,128]{0,1:T(8,128)}), f32[16384,128]{0,1:T(8,128)}) %all-gather.8.cloned.1.call-update) | async-done | bytes 8388624 | tf_op jit(solution)/shard_map/all_gather | solution.py:55
  925.1 11.7 reshape.91
  936.8 9.9 constant_dynamic-slice_fusion.3
  946.7 10.3 copy.28
  956.9 11.8 fusion.5
  968.8 101.8 %reduce-scatter.3.cloned.1.call-done = f32[256,16,256]{2,0,1:T(8,128)} async-done(((f32[256,32,256]{2,0,1:T(8,128)}), f32[256,16,256]{2,0,1:T(8,128)}) %reduce-scatter.3.cloned.1.call-update) | async-done | bytes 4194320 | tf_op jit(solution)/shard_map/reduce_scatter | solution.py:70
  1070.7 111.7 %all-gather.6.cloned.1.call-done = f32[256,32,256]{2,0,1:T(8,128)} async-done(((f32[256,16,256]{2,0,1:T(8,128)}), f32[256,32,256]{2,0,1:T(8,128)}) %all-gather.6.cloned.1.call-update) | async-done | bytes 8388624 | tf_op jit(solution)/shard_map/all_gather | solution.py:76
  1182.4 9.0 copy.30
  1193.6 641.2 %all-reduce.10.cloned.1.call-done = f32[256,256]{0,1:T(8,128)} async-done(((f32[256,256]{0,1:T(8,128)}), f32[256,256]{0,1:T(8,128)}) %all-reduce.10.cloned.1.call-update) | async-done | bytes 262160 | tf_op jit(solution)/shard_map/psum | solution.py:11
  1836.9 11.7 cholesky.164
  1848.7 9.8 custom-call.15
  1859.0 11.7 cholesky.181
  1873.7 4.4 while.5
  1878.0 19.7 custom-call.16
  1900.9 27.1 %all-reduce.12.cloned.1.call-done = f32[256,128]{0,1:T(8,128)} async-done(((f32[256,128]{0,1:T(8,128)}), f32[256,128]{0,1:T(8,128)}) %all-reduce.12.cloned.1.call-update) | async-done | bytes 131088 | tf_op jit(solution)/shard_map/psum | solution.py:11
  1928.0 162.0 %all-gather.10.cloned.1.call-done = f32[16384,128]{0,1:T(8,128)} async-done(((f32[256,128]{0,1:T(8,128)}), f32[16384,128]{0,1:T(8,128)}) %all-gather.10.cloned.1.call-update) | async-done | bytes 8388624 | tf_op jit(solution)/shard_map/all_gather | solution.py:55
  2090.1 11.7 reshape.95
  2101.8 9.9 constant_dynamic-slice_fusion.2
  2111.6 10.3 copy.39
  2121.9 12.0 fusion.3
  2133.9 11.7 copy.50
  2145.8 90.0 %reduce-scatter.5.cloned.1.call-done = f32[256,16,256]{2,0,1:T(8,128)} async-done(((f32[256,32,256]{2,0,1:T(8,128)}), f32[256,16,256]{2,0,1:T(8,128)}) %reduce-scatter.5.cloned.1.call-update) | async-done | bytes 4194320 | tf_op jit(solution)/shard_map/reduce_scatter | solution.py:81
  2235.8 5.6 fusion.2
  2241.4 6.4 copy.41
  (94 shorter events, 26.5 us)
Async XLA Ops:
  6.5 664.1 %all-reduce.6.cloned.1.call-start = ((), (), s32[]{:S(2)}) async-start(), calls=%async_computation.2 | async-start | bytes 524288 | tf_op jit(solution)/shard_map/psum | solution.py:11
  27.7 735.3 %all-reduce.8.cloned.1.call-start = ((), (), s32[]{:S(2)}) async-start(), calls=%async_computation.3 | async-start | bytes 262144 | tf_op jit(solution)/shard_map/psum | solution.py:11
  735.9 189.2 %all-gather.8.cloned.1.call-start = ((), (), s32[]{:S(2)}) async-start(), calls=%async_computation.9 | async-start | bytes 8519680 | tf_op jit(solution)/shard_map/all_gather | solution.py:55
  763.0 307.6 %reduce-scatter.3.cloned.1.call-start = ((), (), s32[]{:S(2)}) async-start(), calls=%async_computation.4 | async-start | bytes 12582912 | tf_op jit(solution)/shard_map/reduce_scatter | solution.py:70
  936.8 20.1 copy-start
  968.7 213.6 %all-gather.6.cloned.1.call-start = ((), (), s32[]{:S(2)}) async-start(), calls=%async_computation.5 | async-start | bytes 12582912 | tf_op jit(solution)/shard_map/all_gather | solution.py:76
  1070.6 764.2 %all-reduce.10.cloned.1.call-start = ((), (), s32[]{:S(2)}) async-start(), calls=%async_computation.6 | async-start | bytes 524288 | tf_op jit(solution)/shard_map/psum | solution.py:11
  1193.1 734.9 %all-reduce.12.cloned.1.call-start = ((), (), s32[]{:S(2)}) async-start(), calls=%async_computation.7 | async-start | bytes 262144 | tf_op jit(solution)/shard_map/psum | solution.py:11
  1900.8 189.2 %all-gather.10.cloned.1.call-start = ((), (), s32[]{:S(2)}) async-start(), calls=%async_computation.10 | async-start | bytes 8519680 | tf_op jit(solution)/shard_map/all_gather | solution.py:55
  1928.0 307.8 %reduce-scatter.5.cloned.1.call-start = ((), (), s32[]{:S(2)}) async-start(), calls=%async_computation.8 | async-start | bytes 12582912 | tf_op jit(solution)/shard_map/reduce_scatter | solution.py:81
  2101.8 20.1 copy-start.1
Sparse Core Ops, SparseCore 0:
  27.8 642.8 all-reduce.5
  736.0 26.9 all-reduce.7
  767.0 158.0 all-gather.7
  968.8 101.7 reduce-scatter.2
  1072.2 110.0 all-gather.5
  1193.2 641.5 all-reduce.9
  1901.0 26.9 all-reduce.11
  1932.0 158.0 all-gather.9
  2134.0 101.7 reduce-scatter.4
where the time goes:
time: 2270 us; the launch traced here: 2250 us
  waiting for transfers between devices  1970 us (87%)
  local copies, waits for them, and re-layouts  121 us (5%)
  other arithmetic  120 us (5%)
  matrix products  29.3 us (1%)
    psum x4, waiting for transfers between devices, from_root(): return lax.psum(jnp.where(mine, shard, jnp.zeros_like(shard)), axis)  1340 us
    all_gather x2, waiting for transfers between devices, on_device(): lax.all_gather(share.reshape(row_blocks, 1, block_size, half), 'row', axi...  324 us
    all_gather x1, waiting for transfers between devices, on_device(): summed = lax.all_gather(shares, 'layer', axis=1, tiled=True)  112 us
    reduce_scatter x1, waiting for transfers between devices, on_device(): lax.psum_scatter(update.reshape(rows, col_blocks, block_size), 'layer', s...  102 us
    reduce_scatter x1, waiting for transfers between devices, on_device(): lax.psum_scatter(total.reshape(rows, col_blocks, block_size), 'layer', sc...  90 us
    another operation x13, other arithmetic, factor_block(): lower_fac = jnp.linalg.cholesky(diag_block)  68.5 us
  transfers between devices with their start and end apart: 9, of which 9 were waited for; matrix products, arithmetic and copies ran while one was open for 1% of the time, Pallas kernels for 0%

commit v1 on v0

v1 whole, which is shorter than its diff:
```python
import jax
import jax.numpy as jnp
from jax import lax
from jax.experimental import pallas as pl
from jax.experimental.pallas import tpu as pltpu
from jax.sharding import PartitionSpec as P

HIGH = lax.Precision.HIGHEST
BS = 256
LEAD = 2 * BS
NB = 128
ZROWS = 88
YROWS = 40
YBASE = 2 * ZROWS
MESH = pl.DeviceIdType.MESH


def dotf(a, b, ca, cb):
    return lax.dot_general(
        a, b, (((ca,), (cb,)), ((), ())), precision=HIGH, preferred_element_type=jnp.float32
    )


def diag_factor(dx, between):
    sub = lax.broadcasted_iota(jnp.int32, (8, NB), 0)
    for p in range(NB // 8):
        lo = 8 * p
        left = dx[lo : lo + 8, 0:NB]
        right = dx[lo : lo + 8, NB : 2 * NB]
        cols = [jnp.broadcast_to(left[:, lo + i : lo + i + 1], (8, NB)) for i in range(8)]
        for i in range(8):
            pivot = jnp.broadcast_to(cols[i][i : i + 1, :], (8, NB))
            root = lax.rsqrt(pivot)
            keep = jnp.where(sub == i, root, 1.0)
            mult = jnp.where(sub > i, cols[i] * (root * root), 0.0)
            for k in range(i + 1, 8):
                row = jnp.broadcast_to(cols[k][i : i + 1, :], (8, NB))
                cols[k] = cols[k] * keep - mult * row
            left = left * keep - mult * jnp.broadcast_to(left[i : i + 1, :], (8, NB))
            right = right * keep - mult * jnp.broadcast_to(right[i : i + 1, :], (8, NB))
        both = jnp.concatenate([left, right], axis=1)
        dx[lo : lo + 8, :] = both
        if p < NB // 8 - 1:
            upd = dotf(left, both, 0, 0)
            dx[lo + 8 :, :] = dx[lo + 8 :, :] - upd[lo + 8 :, :]
        between(p)


def gather_kernel(
    col0, g, q_out, p_out, w, abuf, m, dx,
    inj_send, inj_recv, w_send, w_recv,
    sc_send, sc_recv, ag_send, ag_recv, sib_send, sib_recv,
    z_send, z_recv, yz_send, yz_recv, yy_send, yy_recv, loc,
):
    row = lax.axis_index("row")
    core = lax.axis_index("col")
    xlo = lax.axis_index("layer")
    z = row // 8
    y = (row // 2) % 4
    xhi = row % 2
    x = xhi * 2 + xlo
    n = z * 4 + y

    def dev(dz, dy, dx_, dc):
        return {"row": dz * 8 + dy * 2 + dx_ // 2, "col": dc, "layer": dx_ % 2}

    def remote(src, dst, ss, rs, to):
        return pltpu.make_async_remote_copy(
            src_ref=src, dst_ref=dst, send_sem=ss, recv_sem=rs, device_id=to, device_id_type=MESH
        )

    sibling = dev(z, y, x, 1 - core)

    unit = xhi + core
    is_src = (row < 2) & ((xhi == 0) | (core == 1))
    own_src = (row == 0) & (core == 0)
    match = n % 2 == core

    @pl.when(is_src)
    def _():
        def one(i, _):
            src = col0.at[pl.ds(pl.multiple_of(8 * i, 8), 8), :]
            dst = abuf.at[unit, i // 2, i % 2]

            @pl.when((i == 0) & own_src)
            def _():
                pltpu.make_async_copy(src, dst, sc_recv.at[unit]).start()

            @pl.when(jnp.logical_not((i == 0) & own_src))
            def _():
                remote(src, dst, sc_send.at[0], sc_recv.at[unit], dev(i // 4, i % 4, x, i % 2)).start()

            remote(src, dst, sc_send.at[0], sc_recv.at[unit], dev(i // 4, i % 4, 3 - x, i % 2)).start()
            return 0

        lax.fori_loop(0, 32, one, 0)

    zhalf = z // 4
    same = xlo == zhalf
    inj_x = jnp.where(same, x, 3 - x)
    inj_self = same & (xhi == core)
    own_slot = (z % 4) * 4 + y
    inj_dst = g.at[pl.ds(pl.multiple_of(own_slot * BS, BS), BS), pl.ds(pl.multiple_of(core * BS, BS), BS)]
    inj = remote(col0, inj_dst, inj_send.at[0], inj_recv.at[core], dev(z, y, inj_x, xhi))
    inj_local = pltpu.make_async_copy(col0, inj_dst, inj_recv.at[core])

    @pl.when(inj_self)
    def _():
        inj_local.start()

    @pl.when(jnp.logical_not(inj_self))
    def _():
        inj.start()

    w_copy = remote(col0, w.at[core], w_send.at[0], w_recv.at[0], sibling)
    w_copy.start()
    w_local = pltpu.make_async_copy(col0, w.at[core], loc.at[0])
    w_local.start()

    def spread(which, first, count):
        @pl.when(match)
        def _():
            for u in range(first, first + count):
                pltpu.make_async_copy(
                    abuf.at[u, n // 2, core], abuf.at[u, n // 2, core], sc_recv.at[u]
                ).wait()
            piece = abuf.at[pl.ds(first, count), n // 2, core]

            def one(i, _):
                other = (n + i) % 32
                remote(piece, piece, ag_send.at[which], ag_recv.at[which], dev(other // 4, other % 4, x, core)).start()
                return 0

            lax.fori_loop(1, 32, one, 0)

    spread(0, 0, 1)
    spread(1, 1, 2)

    def bytes_wait(sem, pieces):
        ref = m.at[0 : 8 * pieces, 0:BS]
        pltpu.make_async_copy(ref, ref, sem).wait()

    def sib_copy(which, first, count):
        half = abuf.at[pl.ds(first, count), :, core]
        return remote(half, half, sib_send.at[which], sib_recv.at[which], sibling)

    def lead_half(which, first, count):
        @pl.when(match)
        def _():
            bytes_wait(ag_recv.at[which], 15 * count)

        @pl.when(jnp.logical_not(match))
        def _():
            bytes_wait(ag_recv.at[which], 16 * count)

        sib_copy(which, first, count).start()

    zp = (z + 8 - 4 * xlo) % 8
    near = zp < 4
    far = jnp.logical_not(near)
    zd = (zp, (11 - zp) % 8)
    base = tuple(jnp.where(v < 4, v, 3) for v in zd)
    nsend = tuple(jnp.where((v <= 2) | (v == 7), 3, 4) for v in zd)
    zto = (dev((z + 1) % 8, y, x, core), dev((z + 7) % 8, y, x, core))
    yup = dev(z, (y + 1) % 4, x, core)
    ydown = dev(z, (y + 3) % 4, x, core)
    yto = (yup, ydown)
    yfrom = ((y + 3) % 4, (y + 1) % 4)
    gray = (0, 1, 3, 2)
    yslot = {1: 1, 3: 0, 2: 2}

    def source_z(d, q):
        s = (base[d] + 4 - q) % 4
        return s if d == 0 else 3 - s

    def part(zs, ys, first, rows):
        start = (zs * 4 + ys) * BS + first
        return g.at[pl.ds(pl.multiple_of(start, 8), rows), :]

    def zpart(d, q, ys):
        return part(source_z(d, q), ys, ZROWS * d, ZROWS)

    def ypart(d, zs, ys):
        return part(zs, ys, YBASE + YROWS * d, YROWS)

    def zchunk(d, q, j):
        if j == 0:
            return zpart(d, q, y)
        return ypart(d, source_z(d, q), (y + gray[j - 1]) % 4)

    def zcopy(d, q, j, ref):
        return remote(ref, ref, z_send.at[d, q, j], z_recv.at[d, q, j], zto[d])

    def yz_copy(d, q, s, ref, to):
        return remote(ref, ref, yz_send.at[d, q, s], yz_recv.at[d, q, s], to)

    def yy_copy(d, s, ref, to):
        return remote(ref, ref, yy_send.at[d, s], yy_recv.at[d, s], to)

    def near_start():
        @pl.when(near)
        def _():
            for h in range(2):
                pltpu.make_async_copy(col0, col0, inj_recv.at[h]).wait()
            for d in range(2):
                ref = ypart(d, z % 4, y)
                yy_copy(d, 0, ref, yup).start()
                yy_copy(d, 1, ref, ydown).start()

    def near_forward():
        @pl.when(near)
        def _():
            for d in range(2):
                ref = ypart(d, z % 4, yfrom[d])
                yy_copy(d, d, ref, yto[d]).wait_recv()
                yy_copy(d, 2, ref, yto[d]).start()

    def event(d, q, j):
        ref = zchunk(d, q, j)

        @pl.when(near & (q > 0))
        def _():
            pltpu.make_async_copy(ref, ref, z_recv.at[d, jnp.maximum(q - 1, 0), j]).wait()

        @pl.when(far)
        def _():
            pltpu.make_async_copy(ref, ref, z_recv.at[d, q, j]).wait()

        if j > 1 and yslot[gray[j - 1]] != d:
            @pl.when(near & (q == 0))
            def _():
                pltpu.make_async_copy(ref, ref, yy_recv.at[d, yslot[gray[j - 1]]]).wait()

        @pl.when(q < nsend[d])
        def _():
            zcopy(d, q, j, ref).start()

        if j == 0:
            yz_copy(d, q, 0, ref, yup).start()
            yz_copy(d, q, 1, ref, ydown).start()

    def y_forward(d, q):
        ref = zpart(d, q, yfrom[d])
        yz_copy(d, q, d, ref, yto[d]).wait_recv()
        yz_copy(d, q, 2, ref, yto[d]).start()

    def finish():
        inj_wait = jnp.logical_not(inj_self)

        @pl.when(inj_wait)
        def _():
            inj.wait_send()

        w_copy.wait_send()

        @pl.when(is_src)
        def _():
            @pl.when(own_src)
            def _():
                bytes_wait(sc_send.at[0], 63)

            @pl.when(jnp.logical_not(own_src))
            def _():
                bytes_wait(sc_send.at[0], 64)

        @pl.when(match)
        def _():
            bytes_wait(ag_send.at[0], 31)
            bytes_wait(ag_send.at[1], 62)

        for which, first, count in ((0, 0, 1), (1, 1, 2)):
            sib_copy(which, first, count).wait_send()

        @pl.when(near)
        def _():
            for d in range(2):
                for s in range(3):
                    yy_copy(d, s, ypart(d, z % 4, y), yup).wait_send()

        def each(q, _):
            for d in range(2):
                for s in range(3):
                    copy = yz_copy(d, q, s, zpart(d, q, y), yup)
                    copy.wait_send()
                    if s != d:
                        copy.wait_recv()

                @pl.when(q < nsend[d])
                def _():
                    for j in range(5):
                        zcopy(d, q, j, zchunk(d, q, j)).wait_send()
            return 0

        lax.fori_loop(0, 4, each, 0)

    near_start()

    def comm(q, _):
        for j in range(5):
            for d in range(2):
                event(d, q, j)
            if j == 1:
                @pl.when(q == 0)
                def _():
                    near_forward()
        for d in range(2):
            y_forward(d, q)
        return 0

    lax.fori_loop(0, 4, comm, 0)

    eye = (
        lax.broadcasted_iota(jnp.int32, (LEAD, LEAD), 0)
        == lax.broadcasted_iota(jnp.int32, (LEAD, LEAD), 1)
    ).astype(jnp.float32)
    m[:, LEAD:] = eye
    lead_half(0, 0, 1)
    lead_half(1, 1, 2)
    for which, first, count in ((0, 0, 1), (1, 1, 2)):
        sib_copy(which, first, count).wait_recv()
    m[0:BS, 0:BS] = abuf[0].reshape(BS, BS)
    m[0:BS, BS:LEAD] = abuf[1].reshape(BS, BS)
    m[BS:LEAD, BS:LEAD] = abuf[2].reshape(BS, BS)
    m[BS:LEAD, 0:BS] = jnp.zeros((BS, BS), jnp.float32)

    def step(k, _):
        off = pl.multiple_of(k * NB, NB)
        dx[:, 0:NB] = m[pl.ds(off, NB), pl.ds(off, NB)]
        dx[:, NB : 2 * NB] = eye[0:NB, 0:NB]
        diag_factor(dx, lambda p: None)
        mk = dotf(dx[:, NB : 2 * NB], m[pl.ds(off, NB), :], 1, 0)
        m[pl.ds(off, NB), :] = mk

        def trail(i, _):
            oi = pl.multiple_of(i * NB, NB)
            u = m[pl.ds(off, NB), pl.ds(oi, NB)]
            m[pl.ds(oi, NB), :] = m[pl.ds(oi, NB), :] - dotf(u, mk, 0, 0)
            return 0

        lax.fori_loop(k + 1, LEAD // NB, trail, 0)
        return 0

    lax.fori_loop(0, LEAD // NB, step, 0)

    w_copy.wait_recv()
    w_local.wait()
    p0 = dotf(w[0], m[0:BS, LEAD : LEAD + BS], 1, 1)
    p1 = dotf(w[0], m[BS:LEAD, LEAD : LEAD + BS], 1, 1) + dotf(w[1], m[BS:LEAD, LEAD + BS :], 1, 1)
    q_out[:, 0:BS] = dotf(p0, m[0:BS, LEAD : LEAD + BS], 1, 0) + dotf(p1, m[BS:LEAD, LEAD : LEAD + BS], 1, 0)
    q_out[:, BS:LEAD] = dotf(p1, m[BS:LEAD, LEAD + BS :], 1, 0)
    p_out[...] = jnp.where(core == 0, p0, p1)
    ri = lax.broadcasted_iota(jnp.int32, (BS, BS), 0)
    ci = lax.broadcasted_iota(jnp.int32, (BS, BS), 1)

    @pl.when((row == 0) & (core == 0))
    def _():
        p_out[...] = jnp.where(ri >= ci, m[0:BS, 0:BS].T, 0.0)

    @pl.when((row == 0) & (core == 1))
    def _():
        p_out[...] = jnp.zeros((BS, BS), jnp.float32)

    @pl.when((row == 1) & (core == 0))
    def _():
        p_out[...] = m[0:BS, BS:LEAD].T

    @pl.when((row == 1) & (core == 1))
    def _():
        p_out[...] = jnp.where(ri >= ci, m[BS:LEAD, BS:LEAD].T, 0.0)

    finish()


def gather_and_factor(col0):
    dma = pltpu.SemaphoreType.DMA
    vmem = pl.BlockSpec(memory_space=pltpu.VMEM)
    return pl.pallas_call(
        gather_kernel,
        out_shape=(
            jax.ShapeDtypeStruct((16 * BS, LEAD), jnp.float32),
            jax.ShapeDtypeStruct((BS, LEAD), jnp.float32),
            jax.ShapeDtypeStruct((BS, BS), jnp.float32),
        ),
        in_specs=[vmem],
        out_specs=(pl.BlockSpec(memory_space=pl.ANY), vmem, vmem),
        scratch_shapes=[
            pltpu.VMEM((2, BS, BS), jnp.float32),
            pltpu.VMEM((3, 16, 2, 8, BS), jnp.float32),
            pltpu.VMEM((LEAD, 2 * LEAD), jnp.float32),
            pltpu.VMEM((NB, 2 * NB), jnp.float32),
            dma((1,)), dma((2,)), dma((1,)), dma((1,)),
            dma((1,)), dma((3,)), dma((2,)), dma((2,)), dma((2,)), dma((2,)),
            dma((2, 4, 5)), dma((2, 4, 5)), dma((2, 4, 3)), dma((2, 4, 3)), dma((2, 3)), dma((2, 3)),
            dma((1,)),
        ],
        compiler_params=pltpu.CompilerParams(has_side_effects=True, vmem_limit_bytes=40 << 20),
        cost_estimate=pl.CostEstimate(flops=2 * LEAD**3, bytes_accessed=16 << 20, transcendentals=LEAD),
    )(col0)


def update_kernel(layer, base, g, q, panel, out):
    step = pl.program_id(0)
    for b in range(4):
        upd = dotf(q[...], g[b * BS : (b + 1) * BS, :], 1, 1)
        for h in range(2):
            s = 2 * b + h
            out[:, s, :] = base[:, s, :] - upd[:, h * 128 : (h + 1) * 128]

    @pl.when((step == 0) & (layer[0] == 0))
    def _():
        for h in range(2):
            out[:, h, :] = panel[:, h * 128 : (h + 1) * 128]


def update(layer, tile, g, q, panel):
    return pl.pallas_call(
        update_kernel,
        out_shape=jax.ShapeDtypeStruct((BS, 32, 128), jnp.float32),
        grid_spec=pltpu.PrefetchScalarGridSpec(
            num_scalar_prefetch=1,
            grid=(4,),
            in_specs=[
                pl.BlockSpec((BS, 8, 128), lambda i, lay: (0, lay[0] * 4 + i, 0)),
                pl.BlockSpec((4 * BS, LEAD), lambda i, lay: (i, 0)),
                pl.BlockSpec((BS, LEAD), lambda i, lay: (0, 0)),
                pl.BlockSpec((BS, BS), lambda i, lay: (0, 0)),
            ],
            out_specs=pl.BlockSpec((BS, 8, 128), lambda i, lay: (0, i, 0)),
        ),
        compiler_params=pltpu.CompilerParams(vmem_limit_bytes=40 << 20),
        cost_estimate=pl.CostEstimate(flops=2 * BS * LEAD * 16 * BS, bytes_accessed=16 << 20, transcendentals=0),
    )(layer, tile, g, q, panel)


def on_device(matrix):
    tile = matrix.reshape(BS, 64, 128)
    col0 = tile[:, 0:2, :].reshape(BS, BS)
    g, q, panel = gather_and_factor(col0)
    layer = lax.axis_index("layer").reshape(1).astype(jnp.int32)
    out = update(layer, tile, g, q, panel)
    return out.reshape(1, 1, BS, 16, 1, BS)


def solution(mesh):
    in_specs = (P(None, "row", None, None, "col", None),)
    out_specs = P(None, "row", None, "layer", "col", None)
    return jax.shard_map(
        on_device, mesh=mesh, in_specs=in_specs, out_specs=out_specs, check_vma=False
    )
```

time: 2270 us -> 553 us (0.24)
  waiting for transfers between devices: 1970 us -> 0 us
  Pallas kernels: 0 us -> 536 us
  other arithmetic: 120 us -> 0 us
  local copies, waits for them, and re-layouts: 121 us -> 7.91 us
  matrix products: 29.3 us -> 0 us
    psum x4 -> x0, waiting for transfers between devices: 1340 us -> none  [from_root(): return lax.psum(jnp.where(mine, shard, jnp.zeros_like(shard)), axis)]
    pallas_call x0 -> x2, Pallas kernels: none -> 536 us  [the longest x1 522 us: gather_and_factor(): pl.pallas_call(gather_kernel, out_shape=(jax.ShapeDtypeStruct((16 * BS, L...]
    all_gather x3 -> x0, waiting for transfers between devices: 436 us -> none  [the longest x2 324 us: on_device(): lax.all_gather(share.reshape(row_blocks, 1, block_size, half), 'row', axi...]
    reduce_scatter x2 -> x0, waiting for transfers between devices: 192 us -> none  [the longest x1 102 us: on_device(): lax.psum_scatter(update.reshape(rows, col_blocks, block_size), 'layer', s...]
    another operation x18 -> x0, other arithmetic: 108 us -> none  [the longest x13 68.5 us: factor_block(): lower_fac = jnp.linalg.cholesky(diag_block)]
    dynamic_slice x4 -> x0, local copies, waits for them, and re-layouts: 40.3 us -> none  [on_device(): lax.dynamic_index_in_dim(grouped, grid_col, 1, keepdims=False)]
    reshape x3 -> x0, local copies, waits for them, and re-layouts: 29.8 us -> none  [the longest x2 23.4 us: on_device(): grouped = gathered.reshape(col_blocks, col_total, block_size, half)]
    dot_general x4 -> x0, matrix products: 26.5 us -> none  [the longest x2 23.7 us: on_device(): lax.dot_general(share, picked, (((1,), (1,)), ((), ())), precision=HIGH,...]
  transfers between devices with their start and end apart: 9 -> 0, of which waited for: 9 -> 0; matrix products, arithmetic and copies ran while one was open for 1% -> 0% of each run, Pallas kernels for 0% -> 0%
where the time goes in v1:
time: 553 us; the launch traced here: 544 us
  Pallas kernels  536 us (97%)
  local copies, waits for them, and re-layouts  7.91 us (1%)
    pallas_call x1, Pallas kernels, gather_and_factor(): pl.pallas_call(gather_kernel, out_shape=(jax.ShapeDtypeStruct((16 * BS, L...  522 us
    pallas_call x1, Pallas kernels, update(): pl.pallas_call(update_kernel, out_shape=jax.ShapeDtypeStruct((BS, 32, 128...  14.4 us

profile of v1, /device:TPU:6, one launch (start us, length us, event | category | flops | bytes accessed | tf_op | source)
XLA Modules:
  0.0 544.2 jit_solution(10665617226294318613)
XLA Ops:
  0.0 1.3 slice.4
  1.3 521.8 %shard_map.17 = (f32[4096,512]{1,0:T(8,128)S(1)}, f32[256,512]{1,0:T(8,128)S(1)}, f32[256,256]{1,0:T(8,128)S(1)}) custom-call(f32[256,256]{1,0:T(8,128)S(1)} %bitcast.9), custom_call_target="tpu_custom_call" | custom-call | flops 268435456 | bytes 16777216 | tf_op jit(solution)/shard_map/pallas_call | solution.py:377
  523.2 0.0 copy-start.1
  523.2 3.2 copy-done.1
  526.4 0.0 copy-start
  526.4 3.4 copy-done
  529.8 14.4 %shard_map.18 = f32[256,32,128]{2,1,0:T(8,128)} custom-call(s32[1]{0:T(128)} %bitcast.layer, f32[256,64,128]{2,1,0:T(8,128)S(1)} %bitcast.8, f32[4096,512]{1,0:T(8,128)} %copy-done.1, f32[256,512]{1,0:T(8,128)S(1)} %get-tuple-element.9.q, f32[256,256]{1,0:T(8,128)S(1)} %get-tuple-element.10.panel), custom_call_target="tpu_custom_call" | custom-call | flops 1073741824 | bytes 16777216 | tf_op jit(solution)/shard_map/pallas_call | solution.py:416
  (1 shorter events, 0.0 us)
Async XLA Ops:
  523.2 3.2 copy-start.1
  526.4 3.4 copy-start

commit v2 on v1

--- a/solution.py
+++ b/solution.py
@@ -9,9 +9,11 @@
 BS = 256
 LEAD = 2 * BS
 NB = 128
-ZROWS = 88
-YROWS = 40
-YBASE = 2 * ZROWS
+ZROWS = 40
+YROWS = 48
+YBASE = 4 * ZROWS
+EVENTS = 24
+SLOTS = 32
 MESH = pl.DeviceIdType.MESH
 
 
@@ -166,8 +168,11 @@
     ydown = dev(z, (y + 3) % 4, x, core)
     yto = (yup, ydown)
     yfrom = ((y + 3) % 4, (y + 1) % 4)
-    gray = (0, 1, 3, 2)
-    yslot = {1: 1, 3: 0, 2: 2}
+
+    def lag(v):
+        return jnp.where(v < 4, 0, 2 * (v - 3))
+
+    lags = tuple(lag(v) for v in zd)
 
     def source_z(d, q):
         s = (base[d] + 4 - q) % 4
@@ -177,22 +182,17 @@
         start = (zs * 4 + ys) * BS + first
         return g.at[pl.ds(pl.multiple_of(start, 8), rows), :]
 
-    def zpart(d, q, ys):
-        return part(source_z(d, q), ys, ZROWS * d, ZROWS)
+    def zpart(d, q, j, ys):
+        return part(source_z(d, q), ys, 2 * ZROWS * d + ZROWS * j, ZROWS)
 
     def ypart(d, zs, ys):
         return part(zs, ys, YBASE + YROWS * d, YROWS)
 
-    def zchunk(d, q, j):
-        if j == 0:
-            return zpart(d, q, y)
-        return ypart(d, source_z(d, q), (y + gray[j - 1]) % 4)
-
     def zcopy(d, q, j, ref):
         return remote(ref, ref, z_send.at[d, q, j], z_recv.at[d, q, j], zto[d])
 
-    def yz_copy(d, q, s, ref, to):
-        return remote(ref, ref, yz_send.at[d, q, s], yz_recv.at[d, q, s], to)
+    def yz_copy(d, q, j, s, ref, to):
+        return remote(ref, ref, yz_send.at[d, q, j, s], yz_recv.at[d, q, j, s], to)
 
     def yy_copy(d, s, ref, to):
         return remote(ref, ref, yy_send.at[d, s], yy_recv.at[d, s], to)
@@ -215,34 +215,59 @@
                 yy_copy(d, d, ref, yto[d]).wait_recv()
                 yy_copy(d, 2, ref, yto[d]).start()
 
-    def event(d, q, j):
-        ref = zchunk(d, q, j)
-
-        @pl.when(near & (q > 0))
-        def _():
-            pltpu.make_async_copy(ref, ref, z_recv.at[d, jnp.maximum(q - 1, 0), j]).wait()
-
-        @pl.when(far)
-        def _():
-            pltpu.make_async_copy(ref, ref, z_recv.at[d, q, j]).wait()
-
-        if j > 1 and yslot[gray[j - 1]] != d:
-            @pl.when(near & (q == 0))
+    def pass_on(d, q, j, ref):
+        @pl.when(far | (q > 0))
+        def _():
+            arrived = jnp.where(near, q - 1, q)
+            pltpu.make_async_copy(ref, ref, z_recv.at[d, jnp.maximum(arrived, 0), j]).wait()
+
+        @pl.when(q < nsend[d])
+        def _():
+            zcopy(d, q, j, ref).start()
+
+    def event(d, e):
+        q = e // 6
+        j = e % 6
+
+        @pl.when(j < 2)
+        def _():
+            ref = zpart(d, q, j, y)
+            pass_on(d, q, j, ref)
+            yz_copy(d, q, j, 0, ref, yup).start()
+            yz_copy(d, q, j, 1, ref, ydown).start()
+
+        @pl.when(j >= 2)
+        def _():
+            i = j - 2
+            gray = i + i // 2 - 2 * (i // 3)
+            ref = ypart(d, source_z(d, q), (y + gray) % 4)
+
+            for num, s in ((1, 1), (2, 0), (3, 2)):
+                if s != d:
+                    @pl.when(near & (q == 0) & (i == num))
+                    def _():
+                        pltpu.make_async_copy(ref, ref, yy_recv.at[d, s]).wait()
+
+            pass_on(d, q, j, ref)
+
+        @pl.when((j == 3) | (j == 4))
+        def _():
+            ref = zpart(d, q, j - 3, yfrom[d])
+            yz_copy(d, q, j - 3, d, ref, yto[d]).wait_recv()
+            yz_copy(d, q, j - 3, 2, ref, yto[d]).start()
+
+    def slot(t):
+        for d in range(2):
+            late = jnp.where(t < 6, t, jnp.where(t < 10, -1, t - 4))
+            e = jnp.where(zd[d] == 0, late, t - lags[d])
+
+            @pl.when((e >= 0) & (e < EVENTS))
             def _():
-                pltpu.make_async_copy(ref, ref, yy_recv.at[d, yslot[gray[j - 1]]]).wait()
-
-        @pl.when(q < nsend[d])
-        def _():
-            zcopy(d, q, j, ref).start()
-
-        if j == 0:
-            yz_copy(d, q, 0, ref, yup).start()
-            yz_copy(d, q, 1, ref, ydown).start()
-
-    def y_forward(d, q):
-        ref = zpart(d, q, yfrom[d])
-        yz_copy(d, q, d, ref, yto[d]).wait_recv()
-        yz_copy(d, q, 2, ref, yto[d]).start()
+                event(d, e)
+
+        @pl.when(t == 2)
+        def _():
+            near_forward()
 
     def finish():
         inj_wait = jnp.logical_not(inj_self)
@@ -279,35 +304,25 @@
 
         def each(q, _):
             for d in range(2):
-                for s in range(3):
-                    copy = yz_copy(d, q, s, zpart(d, q, y), yup)
-                    copy.wait_send()
-                    if s != d:
-                        copy.wait_recv()
+                for j in range(2):
+                    for s in range(3):
+                        copy = yz_copy(d, q, j, s, zpart(d, q, j, y), yup)
+                        copy.wait_send()
+                        if s != d:
+                            copy.wait_recv()
 
                 @pl.when(q < nsend[d])
                 def _():
-                    for j in range(5):
-                        zcopy(d, q, j, zchunk(d, q, j)).wait_send()
+                    for j in range(6):
+                        ref = zpart(d, q, j, y) if j < 2 else ypart(d, source_z(d, q), y)
+                        zcopy(d, q, j, ref).wait_send()
             return 0
 
         lax.fori_loop(0, 4, each, 0)
 
     near_start()
 
-    def comm(q, _):
-        for j in range(5):
-            for d in range(2):
-                event(d, q, j)
-            if j == 1:
-                @pl.when(q == 0)
-                def _():
-                    near_forward()
-        for d in range(2):
-            y_forward(d, q)
-        return 0
-
-    lax.fori_loop(0, 4, comm, 0)
+    lax.fori_loop(0, SLOTS, lambda t, _: (slot(t), 0)[1], 0)
 
     eye = (
         lax.broadcasted_iota(jnp.int32, (LEAD, LEAD), 0)
@@ -390,7 +405,7 @@
             pltpu.VMEM((NB, 2 * NB), jnp.float32),
             dma((1,)), dma((2,)), dma((1,)), dma((1,)),
             dma((1,)), dma((3,)), dma((2,)), dma((2,)), dma((2,)), dma((2,)),
-            dma((2, 4, 5)), dma((2, 4, 5)), dma((2, 4, 3)), dma((2, 4, 3)), dma((2, 3)), dma((2, 3)),
+            dma((2, 4, 6)), dma((2, 4, 6)), dma((2, 4, 2, 3)), dma((2, 4, 2, 3)), dma((2, 3)), dma((2, 3)),
             dma((1,)),
         ],
         compiler_params=pltpu.CompilerParams(has_side_effects=True, vmem_limit_bytes=40 << 20),

time: 553 us -> 166 us (0.30); the launches traced: 544 us -> 164 us
  Pallas kernels: 536 us -> 156 us
    pallas_call x1, Pallas kernels: 522 us -> 142 us  [gather_and_factor(): pl.pallas_call(gather_kernel, out_shape=(jax.ShapeDtypeStruct((16 * BS, L...]
where the time goes in v2:
time: 166 us; the launch traced here: 164 us
  Pallas kernels  156 us (94%)
  local copies, waits for them, and re-layouts  7.91 us (5%)
    pallas_call x1, Pallas kernels, gather_and_factor(): pl.pallas_call(gather_kernel, out_shape=(jax.ShapeDtypeStruct((16 * BS, L...  142 us
    pallas_call x1, Pallas kernels, update(): pl.pallas_call(update_kernel, out_shape=jax.ShapeDtypeStruct((BS, 32, 128...  14.4 us
    unnamed x5, local copies, waits for them, and re-layouts  6.62 us

profile of v2, /device:TPU:6, one launch (start us, length us, event | category | flops | bytes accessed | tf_op | source)
XLA Modules:
  0.0 164.0 jit_solution(7233315084699191945)
XLA Ops:
  0.0 1.3 slice.4
  1.3 141.6 %shard_map.17 = (f32[4096,512]{1,0:T(8,128)S(1)}, f32[256,512]{1,0:T(8,128)S(1)}, f32[256,256]{1,0:T(8,128)S(1)}) custom-call(f32[256,256]{1,0:T(8,128)S(1)} %bitcast.9), custom_call_target="tpu_custom_call" | custom-call | flops 268435456 | bytes 16777216 | tf_op jit(solution)/shard_map/pallas_call | solution.py:392
  142.9 0.0 copy-start.1
  142.9 3.2 %copy-done.1 = f32[4096,512]{1,0:T(8,128)} copy-done((f32[4096,512]{1,0:T(8,128)}, f32[4096,512]{1,0:T(8,128)S(1)}, u32[]{:S(2)}) %copy-start.1) | copy-done | bytes 8388632
  146.2 0.0 copy-start
  146.2 3.4 %copy-done = f32[1,1,256,32,1,256]{5,4,3,2,1,0:T(1,128)S(1)} copy-done((f32[1,1,256,32,1,256]{5,4,3,2,1,0:T(1,128)S(1)}, f32[1,1,256,32,1,256]{5,4,3,2,1,0:T(1,128)}, u32[]{:S(2)}) %copy-start) | copy-done | bytes 8388632
  149.5 14.4 %shard_map.18 = f32[256,32,128]{2,1,0:T(8,128)} custom-call(s32[1]{0:T(128)} %bitcast.layer, f32[256,64,128]{2,1,0:T(8,128)S(1)} %bitcast.8, f32[4096,512]{1,0:T(8,128)} %copy-done.1, f32[256,512]{1,0:T(8,128)S(1)} %get-tuple-element.9.q, f32[256,256]{1,0:T(8,128)S(1)} %get-tuple-element.10.panel), custom_call_target="tpu_custom_call" | custom-call | flops 1073741824 | bytes 16777216 | tf_op jit(solution)/shard_map/pallas_call | solution.py:431
  (1 shorter events, 0.0 us)
Async XLA Ops:
  142.9 3.2 %copy-start.1 = (f32[4096,512]{1,0:T(8,128)}, f32[4096,512]{1,0:T(8,128)S(1)}, u32[]{:S(2)}) copy-start(f32[4096,512]{1,0:T(8,128)S(1)} %get-tuple-element.8.g) | copy-start | bytes 25165828
  146.2 3.4 %copy-start = (f32[1,1,256,32,1,256]{5,4,3,2,1,0:T(1,128)S(1)}, f32[1,1,256,32,1,256]{5,4,3,2,1,0:T(1,128)}, u32[]{:S(2)}) copy-start(f32[1,1,256,32,1,256]{5,4,3,2,1,0:T(1,128)} %param.1) | copy-start | bytes 25165828

commit v3 on v2

--- a/solution.py
+++ b/solution.py
@@ -11,9 +11,11 @@
 NB = 128
 ZROWS = 40
 YROWS = 48
-YBASE = 4 * ZROWS
+YBASE = 2 * ZROWS
 EVENTS = 24
+PIECE = 16
 SLOTS = 32
+FIRST = 4
 MESH = pl.DeviceIdType.MESH
 
 
@@ -49,7 +51,7 @@
 
 
 def gather_kernel(
-    col0, g, q_out, p_out, w, abuf, m, dx,
+    col0, tile, out, g, q_out, p_out, w, abuf, m, dx,
     inj_send, inj_recv, w_send, w_recv,
     sc_send, sc_recv, ag_send, ag_recv, sib_send, sib_recv,
     z_send, z_recv, yz_send, yz_recv, yy_send, yy_recv, loc,
@@ -76,29 +78,78 @@
     unit = xhi + core
     is_src = (row < 2) & ((xhi == 0) | (core == 1))
     own_src = (row == 0) & (core == 0)
-    match = n % 2 == core
-
-    @pl.when(is_src)
-    def _():
-        def one(i, _):
-            src = col0.at[pl.ds(pl.multiple_of(8 * i, 8), 8), :]
-            dst = abuf.at[unit, i // 2, i % 2]
-
-            @pl.when((i == 0) & own_src)
-            def _():
-                pltpu.make_async_copy(src, dst, sc_recv.at[unit]).start()
-
-            @pl.when(jnp.logical_not((i == 0) & own_src))
-            def _():
-                remote(src, dst, sc_send.at[0], sc_recv.at[unit], dev(i // 4, i % 4, x, i % 2)).start()
-
-            remote(src, dst, sc_send.at[0], sc_recv.at[unit], dev(i // 4, i % 4, 3 - x, i % 2)).start()
-            return 0
-
-        lax.fori_loop(0, 32, one, 0)
-
+    match = (n % 2 == 0) & ((n // 2) % 2 == core)
     zhalf = z // 4
     same = xlo == zhalf
+    ring = (
+        dev((z + 1) % 8, y, x, core),
+        dev((z + 7) % 8, y, x, core),
+        dev(z, (y + 1) % 4, x, core),
+        dev(z, (y + 3) % 4, x, core),
+    )
+
+    barrier = pltpu.get_barrier_semaphore()
+
+    def greet(to):
+        pl.semaphore_signal(barrier, inc=1, device_id=to, device_id_type=MESH)
+
+    for to in ring + (sibling,):
+        greet(to)
+
+    @pl.when(match)
+    def _():
+        low = jnp.where(xhi == 0, x, 3 - x)
+
+        @pl.when(jnp.logical_not(own_src))
+        def _():
+            greet(dev(0, 0, low, 0))
+
+        greet(dev(0, 0, low, 1))
+        greet(dev(0, 0, 3 - low, 1))
+
+    @pl.when(same & (core != xhi))
+    def _():
+        greet(dev(z, y, 3 - x, 0))
+        greet(dev(z, y, 3 - x, 1))
+
+    def greet_holder(i, _):
+        holder = 4 * i + 2 * core
+
+        @pl.when(holder != n)
+        def _():
+            greet(dev(holder // 4, holder % 4, x, core))
+
+        return 0
+
+    lax.fori_loop(0, 8, greet_holder, 0)
+    pl.semaphore_wait(
+        barrier,
+        5
+        + jnp.where(match, 31, 0)
+        + jnp.where(is_src, 32, 0)
+        - jnp.where(own_src, 1, 0)
+        + jnp.where(same, 0, 1),
+    )
+
+    @pl.when(is_src)
+    def _():
+        for i in range(16):
+            src = col0.at[PIECE * i : PIECE * (i + 1), :]
+            dst = abuf.at[unit, i // 2, i % 2]
+            hz, hy = i // 2, 2 * (i % 2)
+            here = remote(src, dst, sc_send.at[0], sc_recv.at[unit], dev(hz, hy, x, i % 2))
+            if i == 0:
+                @pl.when(own_src)
+                def _():
+                    pltpu.make_async_copy(src, dst, sc_recv.at[unit]).start()
+
+                @pl.when(jnp.logical_not(own_src))
+                def _():
+                    here.start()
+            else:
+                here.start()
+            remote(src, dst, sc_send.at[0], sc_recv.at[unit], dev(hz, hy, 3 - x, i % 2)).start()
+
     inj_x = jnp.where(same, x, 3 - x)
     inj_self = same & (xhi == core)
     own_slot = (z % 4) * 4 + y
@@ -118,15 +169,17 @@
     w_copy.start()
     w_local = pltpu.make_async_copy(col0, w.at[core], loc.at[0])
     w_local.start()
+    tile_copy = pltpu.make_async_copy(tile.at[:, pl.ds(pl.multiple_of(xlo * 32, 32), 32), :], out, loc.at[1])
+    tile_copy.start()
 
     def spread(which, first, count):
         @pl.when(match)
         def _():
             for u in range(first, first + count):
                 pltpu.make_async_copy(
-                    abuf.at[u, n // 2, core], abuf.at[u, n // 2, core], sc_recv.at[u]
+                    abuf.at[u, n // 4, core], abuf.at[u, n // 4, core], sc_recv.at[u]
                 ).wait()
-            piece = abuf.at[pl.ds(first, count), n // 2, core]
+            piece = abuf.at[pl.ds(first, count), n // 4, core]
 
             def one(i, _):
                 other = (n + i) % 32
@@ -135,11 +188,9 @@
 
             lax.fori_loop(1, 32, one, 0)
 
-    spread(0, 0, 1)
-    spread(1, 1, 2)
 
     def bytes_wait(sem, pieces):
-        ref = m.at[0 : 8 * pieces, 0:BS]
+        ref = m.at[0 : 8 * pieces, 0:LEAD]
         pltpu.make_async_copy(ref, ref, sem).wait()
 
     def sib_copy(which, first, count):
@@ -149,11 +200,11 @@
     def lead_half(which, first, count):
         @pl.when(match)
         def _():
-            bytes_wait(ag_recv.at[which], 15 * count)
+            bytes_wait(ag_recv.at[which], 7 * count)
 
         @pl.when(jnp.logical_not(match))
         def _():
-            bytes_wait(ag_recv.at[which], 16 * count)
+            bytes_wait(ag_recv.at[which], 8 * count)
 
         sib_copy(which, first, count).start()
 
@@ -183,10 +234,10 @@
         return g.at[pl.ds(pl.multiple_of(start, 8), rows), :]
 
     def zpart(d, q, j, ys):
-        return part(source_z(d, q), ys, 2 * ZROWS * d + ZROWS * j, ZROWS)
+        return part(source_z(d, q), ys, NB * d + ZROWS * j, ZROWS)
 
     def ypart(d, zs, ys):
-        return part(zs, ys, YBASE + YROWS * d, YROWS)
+        return part(zs, ys, NB * d + YBASE, YROWS)
 
     def zcopy(d, q, j, ref):
         return remote(ref, ref, z_send.at[d, q, j], z_recv.at[d, q, j], zto[d])
@@ -257,6 +308,7 @@
             yz_copy(d, q, j - 3, 2, ref, yto[d]).start()
 
     def slot(t):
+        t = jnp.int32(t)
         for d in range(2):
             late = jnp.where(t < 6, t, jnp.where(t < 10, -1, t - 4))
             e = jnp.where(zd[d] == 0, late, t - lags[d])
@@ -265,7 +317,7 @@
             def _():
                 event(d, e)
 
-        @pl.when(t == 2)
+        @pl.when(jnp.int32(t) == 2)
         def _():
             near_forward()
 
@@ -282,11 +334,11 @@
         def _():
             @pl.when(own_src)
             def _():
-                bytes_wait(sc_send.at[0], 63)
+                bytes_wait(sc_send.at[0], 31)
 
             @pl.when(jnp.logical_not(own_src))
             def _():
-                bytes_wait(sc_send.at[0], 64)
+                bytes_wait(sc_send.at[0], 32)
 
         @pl.when(match)
         def _():
@@ -308,8 +360,6 @@
                     for s in range(3):
                         copy = yz_copy(d, q, j, s, zpart(d, q, j, y), yup)
                         copy.wait_send()
-                        if s != d:
-                            copy.wait_recv()
 
                 @pl.when(q < nsend[d])
                 def _():
@@ -321,28 +371,41 @@
         lax.fori_loop(0, 4, each, 0)
 
     near_start()
-
-    lax.fori_loop(0, SLOTS, lambda t, _: (slot(t), 0)[1], 0)
+    slot(0)
+    spread(0, 0, 1)
+    spread(1, 1, 2)
+    slot(1)
+    lead_half(0, 0, 1)
+    slot(2)
+    lead_half(1, 1, 2)
+    slot(3)
 
     eye = (
         lax.broadcasted_iota(jnp.int32, (LEAD, LEAD), 0)
         == lax.broadcasted_iota(jnp.int32, (LEAD, LEAD), 1)
     ).astype(jnp.float32)
     m[:, LEAD:] = eye
-    lead_half(0, 0, 1)
-    lead_half(1, 1, 2)
-    for which, first, count in ((0, 0, 1), (1, 1, 2)):
-        sib_copy(which, first, count).wait_recv()
+    sib_copy(0, 0, 1).wait_recv()
     m[0:BS, 0:BS] = abuf[0].reshape(BS, BS)
-    m[0:BS, BS:LEAD] = abuf[1].reshape(BS, BS)
-    m[BS:LEAD, BS:LEAD] = abuf[2].reshape(BS, BS)
     m[BS:LEAD, 0:BS] = jnp.zeros((BS, BS), jnp.float32)
 
     def step(k, _):
         off = pl.multiple_of(k * NB, NB)
         dx[:, 0:NB] = m[pl.ds(off, NB), pl.ds(off, NB)]
         dx[:, NB : 2 * NB] = eye[0:NB, 0:NB]
-        diag_factor(dx, lambda p: None)
+
+        def between(p):
+            if p % 3 == 0 and p < 15:
+                slot(FIRST + 5 * k + p // 3)
+
+        diag_factor(dx, between)
+
+        @pl.when(k == 0)
+        def _():
+            sib_copy(1, 1, 2).wait_recv()
+            m[0:BS, BS:LEAD] = abuf[1].reshape(BS, BS)
+            m[BS:LEAD, BS:LEAD] = abuf[2].reshape(BS, BS)
+
         mk = dotf(dx[:, NB : 2 * NB], m[pl.ds(off, NB), :], 1, 0)
         m[pl.ds(off, NB), :] = mk
 
@@ -357,12 +420,14 @@
 
     lax.fori_loop(0, LEAD // NB, step, 0)
 
+    slot(FIRST + 20)
     w_copy.wait_recv()
     w_local.wait()
     p0 = dotf(w[0], m[0:BS, LEAD : LEAD + BS], 1, 1)
     p1 = dotf(w[0], m[BS:LEAD, LEAD : LEAD + BS], 1, 1) + dotf(w[1], m[BS:LEAD, LEAD + BS :], 1, 1)
     q_out[:, 0:BS] = dotf(p0, m[0:BS, LEAD : LEAD + BS], 1, 0) + dotf(p1, m[BS:LEAD, LEAD : LEAD + BS], 1, 0)
     q_out[:, BS:LEAD] = dotf(p1, m[BS:LEAD, LEAD + BS :], 1, 0)
+    slot(FIRST + 21)
     p_out[...] = jnp.where(core == 0, p0, p1)
     ri = lax.broadcasted_iota(jnp.int32, (BS, BS), 0)
     ci = lax.broadcasted_iota(jnp.int32, (BS, BS), 1)
@@ -383,77 +448,78 @@
     def _():
         p_out[...] = jnp.where(ri >= ci, m[BS:LEAD, BS:LEAD].T, 0.0)
 
+    tile_copy.wait()
+    flat = out.reshape(BS * 32, NB)
+
+    def work(i, _):
+        q = i // 2
+
+        @pl.when(i % 2 == 0)
+        def _():
+            for d in range(2):
+                for j in range(2):
+                    for s in range(3):
+                        if s != d:
+                            yz_copy(d, q, j, s, zpart(d, q, j, y), yup).wait_recv()
+
+        for d in range(2):
+            ids = [(source_z(d, q) * 4 + 2 * (i % 2) + h) * 2 + d for h in range(2)]
+            rows = [g[pl.ds(pl.multiple_of(v * NB, NB), NB), :] for v in ids]
+            upd = dotf(q_out[...], jnp.concatenate(rows, axis=0), 1, 1)
+            for h in range(2):
+                where = pl.ds(ids[h], BS, stride=32)
+                flat[where, :] = flat[where, :] - upd[:, h * NB : (h + 1) * NB]
+        return 0
+
+    def slot_and_work(i, _):
+        slot(FIRST + 22 + i)
+        return work(i, 0)
+
+    lax.fori_loop(0, 6, slot_and_work, 0)
+    lax.fori_loop(6, 8, work, 0)
+
+    @pl.when(xlo == 0)
+    def _():
+        for h in range(2):
+            out[:, h, :] = p_out[:, h * NB : (h + 1) * NB]
+
     finish()
 
 
-def gather_and_factor(col0):
+def factor_and_update(col0, tile):
     dma = pltpu.SemaphoreType.DMA
     vmem = pl.BlockSpec(memory_space=pltpu.VMEM)
     return pl.pallas_call(
         gather_kernel,
-        out_shape=(
-            jax.ShapeDtypeStruct((16 * BS, LEAD), jnp.float32),
-            jax.ShapeDtypeStruct((BS, LEAD), jnp.float32),
-            jax.ShapeDtypeStruct((BS, BS), jnp.float32),
-        ),
-        in_specs=[vmem],
-        out_specs=(pl.BlockSpec(memory_space=pl.ANY), vmem, vmem),
+        out_shape=jax.ShapeDtypeStruct((BS, 32, NB), jnp.float32),
+        in_specs=[vmem, pl.BlockSpec(memory_space=pl.ANY)],
+        out_specs=vmem,
         scratch_shapes=[
+            pltpu.VMEM((16 * BS, LEAD), jnp.float32),
+            pltpu.VMEM((BS, LEAD), jnp.float32),
+            pltpu.VMEM((BS, BS), jnp.float32),
             pltpu.VMEM((2, BS, BS), jnp.float32),
-            pltpu.VMEM((3, 16, 2, 8, BS), jnp.float32),
+            pltpu.VMEM((3, 8, 2, PIECE, BS), jnp.float32),
             pltpu.VMEM((LEAD, 2 * LEAD), jnp.float32),
             pltpu.VMEM((NB, 2 * NB), jnp.float32),
             dma((1,)), dma((2,)), dma((1,)), dma((1,)),
             dma((1,)), dma((3,)), dma((2,)), dma((2,)), dma((2,)), dma((2,)),
             dma((2, 4, 6)), dma((2, 4, 6)), dma((2, 4, 2, 3)), dma((2, 4, 2, 3)), dma((2, 3)), dma((2, 3)),
-            dma((1,)),
+            dma((2,)),
         ],
-        compiler_params=pltpu.CompilerParams(has_side_effects=True, vmem_limit_bytes=40 << 20),
-        cost_estimate=pl.CostEstimate(flops=2 * LEAD**3, bytes_accessed=16 << 20, transcendentals=LEAD),
-    )(col0)
-
-
-def update_kernel(layer, base, g, q, panel, out):
-    step = pl.program_id(0)
-    for b in range(4):
-        upd = dotf(q[...], g[b * BS : (b + 1) * BS, :], 1, 1)
-        for h in range(2):
-            s = 2 * b + h
-            out[:, s, :] = base[:, s, :] - upd[:, h * 128 : (h + 1) * 128]
-
-    @pl.when((step == 0) & (layer[0] == 0))
-    def _():
-        for h in range(2):
-            out[:, h, :] = panel[:, h * 128 : (h + 1) * 128]
-
-
-def update(layer, tile, g, q, panel):
-    return pl.pallas_call(
-        update_kernel,
-        out_shape=jax.ShapeDtypeStruct((BS, 32, 128), jnp.float32),
-        grid_spec=pltpu.PrefetchScalarGridSpec(
-            num_scalar_prefetch=1,
-            grid=(4,),
-            in_specs=[
-                pl.BlockSpec((BS, 8, 128), lambda i, lay: (0, lay[0] * 4 + i, 0)),
-                pl.BlockSpec((4 * BS, LEAD), lambda i, lay: (i, 0)),
-                pl.BlockSpec((BS, LEAD), lambda i, lay: (0, 0)),
-                pl.BlockSpec((BS, BS), lambda i, lay: (0, 0)),
-            ],
-            out_specs=pl.BlockSpec((BS, 8, 128), lambda i, lay: (0, i, 0)),
+        compiler_params=pltpu.CompilerParams(
+            has_side_effects=True, collective_id=0, vmem_limit_bytes=46 << 20
         ),
-        compiler_params=pltpu.CompilerParams(vmem_limit_bytes=40 << 20),
-        cost_estimate=pl.CostEstimate(flops=2 * BS * LEAD * 16 * BS, bytes_accessed=16 << 20, transcendentals=0),
-    )(layer, tile, g, q, panel)
+        cost_estimate=pl.CostEstimate(
+            flops=2 * BS * LEAD * 16 * BS, bytes_accessed=16 << 20, transcendentals=LEAD
+        ),
+    )(col0, tile)
 
 
 def on_device(matrix):
-    tile = matrix.reshape(BS, 64, 128)
+    tile = matrix.reshape(BS, 64, NB)
     col0 = tile[:, 0:2, :].reshape(BS, BS)
-    g, q, panel = gather_and_factor(col0)
-    layer = lax.axis_index("layer").reshape(1).astype(jnp.int32)
-    out = update(layer, tile, g, q, panel)
-    return out.reshape(1, 1, BS, 16, 1, BS)
+    return factor_and_update(col0, tile).reshape(1, 1, BS, 16, 1, BS)
 
 
 def solution(mesh):

time: 166 us -> 121 us (0.73)
  Pallas kernels: 156 us -> 117 us
  local copies, waits for them, and re-layouts: 7.91 us -> 3.33 us
    pallas_call x2 -> x1, Pallas kernels: 156 us -> 117 us  [factor_and_update(): pl.pallas_call(gather_kernel, out_shape=jax.ShapeDtypeStruct((BS, 32, NB)...]
    unnamed x5 -> x2, local copies, waits for them, and re-layouts: 6.62 us -> 2.03 us
where the time goes in v3:
time: 121 us; the launch traced here: 120 us
  Pallas kernels  117 us (97%)
  local copies, waits for them, and re-layouts  3.33 us (3%)
    pallas_call x1, Pallas kernels, factor_and_update(): pl.pallas_call(gather_kernel, out_shape=jax.ShapeDtypeStruct((BS, 32, NB)...  117 us

profile of v3, /device:TPU:6, one launch (start us, length us, event | category | flops | bytes accessed | tf_op | source)
XLA Modules:
  0.0 120.0 jit_solution(2419318866723468363)
XLA Ops:
  0.0 1.3 %slice.4 = f32[256,2,128]{2,1,0:T(2,128)S(1)} slice(f32[256,64,128]{2,1,0:T(8,128)} %bitcast.8), slice={[0:256], [0:2], [0:128]} | slice | bytes 524288 | tf_op jit(solution)/shard_map/slice | solution.py:521
  1.3 116.7 %shard_map.17 = f32[256,32,128]{2,1,0:T(8,128)S(1)} custom-call(f32[256,256]{1,0:T(8,128)S(1)} %bitcast.7, f32[256,64,128]{2,1,0:T(8,128)} %bitcast.9), custom_call_target="tpu_custom_call" | custom-call | flops 1073741824 | bytes 16777216 | tf_op jit(solution)/shard_map/pallas_call | solution.py:492
  118.0 2.0 %copy.7 = f32[1,1,256,16,1,256]{5,4,3,2,1,0:T(1,128)} copy(f32[1,1,256,16,1,256]{5,4,3,2,1,0:T(1,128)S(1)} %bitcast.6) | data formatting | bytes 8388608
  (1 shorter events, 0.0 us)

commit v4 on v3

--- a/solution.py
+++ b/solution.py
@@ -14,7 +14,9 @@
 YBASE = 2 * ZROWS
 EVENTS = 24
 PIECE = 16
-SLOTS = 32
+YWAIT = ((1, 2), (0, 2))
+LAG = 3
+SLOTS = EVENTS + 4 * LAG
 FIRST = 4
 MESH = pl.DeviceIdType.MESH
 
@@ -25,36 +27,79 @@
     )
 
 
+def parts(v):
+    high = v.astype(jnp.bfloat16).astype(jnp.float32)
+    rest = v - high
+    mid = rest.astype(jnp.bfloat16).astype(jnp.float32)
+    low = (rest - mid).astype(jnp.bfloat16).astype(jnp.float32)
+    return high, mid, low
+
+
+def rank8(left, both):
+    a, b, c = parts(left)
+    d, e, f = parts(both)
+    return lax.dot_general(
+        jnp.concatenate([a, a, b, a, c, b], axis=0),
+        jnp.concatenate([d, e, d, f, d, e], axis=0),
+        (((0,), (0,)), ((), ())),
+        preferred_element_type=jnp.float32,
+    )
+
+
+def down(v, i):
+    return jnp.broadcast_to(v[i : i + 1, :], (8, NB))
+
+
+def across(v, j):
+    return jnp.broadcast_to(v[:, j : j + 1], (8, NB))
+
+
 def diag_factor(dx, between):
     sub = lax.broadcasted_iota(jnp.int32, (8, NB), 0)
+    left = dx[0:8, 0:NB]
+    right = dx[0:8, NB : 2 * NB]
     for p in range(NB // 8):
         lo = 8 * p
-        left = dx[lo : lo + 8, 0:NB]
-        right = dx[lo : lo + 8, NB : 2 * NB]
-        cols = [jnp.broadcast_to(left[:, lo + i : lo + i + 1], (8, NB)) for i in range(8)]
+        ahead = p < NB // 8 - 1
+        cols = [across(left, lo + i) for i in range(8)]
+        if ahead:
+            left2 = dx[lo + 8 : lo + 16, 0:NB]
+            right2 = dx[lo + 8 : lo + 16, NB : 2 * NB]
+            cols2 = [across(left2, lo + i) for i in range(8)]
+        scale = None
         for i in range(8):
-            pivot = jnp.broadcast_to(cols[i][i : i + 1, :], (8, NB))
-            root = lax.rsqrt(pivot)
-            keep = jnp.where(sub == i, root, 1.0)
-            mult = jnp.where(sub > i, cols[i] * (root * root), 0.0)
+            root = lax.rsqrt(down(cols[i], i))
+            inv = root * root
+            scale = root if scale is None else jnp.where(sub == i, root, scale)
+            below = jnp.where(sub > i, cols[i], 0.0)
             for k in range(i + 1, 8):
-                row = jnp.broadcast_to(cols[k][i : i + 1, :], (8, NB))
-                cols[k] = cols[k] * keep - mult * row
-            left = left * keep - mult * jnp.broadcast_to(left[i : i + 1, :], (8, NB))
-            right = right * keep - mult * jnp.broadcast_to(right[i : i + 1, :], (8, NB))
-        both = jnp.concatenate([left, right], axis=1)
+                row = down(cols[k], i) * inv
+                cols[k] = cols[k] - below * row
+                if ahead:
+                    cols2[k] = cols2[k] - cols2[i] * row
+            row_l = down(left, i) * inv
+            row_r = down(right, i) * inv
+            left = left - below * row_l
+            right = right - below * row_r
+            if ahead:
+                left2 = left2 - cols2[i] * row_l
+                right2 = right2 - cols2[i] * row_r
+        left = left * scale
+        both = jnp.concatenate([left, right * scale], axis=1)
         dx[lo : lo + 8, :] = both
-        if p < NB // 8 - 1:
-            upd = dotf(left, both, 0, 0)
-            dx[lo + 8 :, :] = dx[lo + 8 :, :] - upd[lo + 8 :, :]
+        if lo + 16 < NB:
+            upd = rank8(left, both)
+            dx[lo + 16 :, :] = dx[lo + 16 :, :] - upd[lo + 16 :, :]
+        if ahead:
+            left, right = left2, right2
         between(p)
 
 
 def gather_kernel(
-    col0, tile, out, g, q_out, p_out, w, abuf, m, dx,
+    col0, tile, out, g, q_out, p_out, w, abuf, m, dx, raw, own,
     inj_send, inj_recv, w_send, w_recv,
     sc_send, sc_recv, ag_send, ag_recv, sib_send, sib_recv,
-    z_send, z_recv, yz_send, yz_recv, yy_send, yy_recv, loc,
+    z_send, z_recv, yz_send, yz_recv, yy_send, yy_recv, x_send, x_recv, loc,
 ):
     row = lax.axis_index("row")
     core = lax.axis_index("col")
@@ -66,7 +111,8 @@
     n = z * 4 + y
 
     def dev(dz, dy, dx_, dc):
-        return {"row": dz * 8 + dy * 2 + dx_ // 2, "col": dc, "layer": dx_ % 2}
+        high = jnp.where(dx_ >= 2, 1, 0)
+        return {"row": dz * 8 + dy * 2 + high, "col": dc, "layer": dx_ - 2 * high}
 
     def remote(src, dst, ss, rs, to):
         return pltpu.make_async_remote_copy(
@@ -93,7 +139,9 @@
     def greet(to):
         pl.semaphore_signal(barrier, inc=1, device_id=to, device_id_type=MESH)
 
-    for to in ring + (sibling,):
+    twin = dev(z, y, (x + 2) % 4, core)
+    native = core == xhi
+    for to in ring + (sibling, twin):
         greet(to)
 
     @pl.when(match)
@@ -124,7 +172,7 @@
     lax.fori_loop(0, 8, greet_holder, 0)
     pl.semaphore_wait(
         barrier,
-        5
+        6
         + jnp.where(match, 31, 0)
         + jnp.where(is_src, 32, 0)
         - jnp.where(own_src, 1, 0)
@@ -152,7 +200,8 @@
 
     inj_x = jnp.where(same, x, 3 - x)
     inj_self = same & (xhi == core)
-    own_slot = (z % 4) * 4 + y
+    zown = z % 4
+    own_slot = zown * 4 + y
     inj_dst = g.at[pl.ds(pl.multiple_of(own_slot * BS, BS), BS), pl.ds(pl.multiple_of(core * BS, BS), BS)]
     inj = remote(col0, inj_dst, inj_send.at[0], inj_recv.at[core], dev(z, y, inj_x, xhi))
     inj_local = pltpu.make_async_copy(col0, inj_dst, inj_recv.at[core])
@@ -169,7 +218,7 @@
     w_copy.start()
     w_local = pltpu.make_async_copy(col0, w.at[core], loc.at[0])
     w_local.start()
-    tile_copy = pltpu.make_async_copy(tile.at[:, pl.ds(pl.multiple_of(xlo * 32, 32), 32), :], out, loc.at[1])
+    tile_copy = pltpu.make_async_copy(tile.at[:, pl.ds(pl.multiple_of(xlo * 32, 32), 32), :], raw, loc.at[1])
     tile_copy.start()
 
     def spread(which, first, count):
@@ -220,13 +269,17 @@
     yto = (yup, ydown)
     yfrom = ((y + 3) % 4, (y + 1) % 4)
 
-    def lag(v):
-        return jnp.where(v < 4, 0, 2 * (v - 3))
-
-    lags = tuple(lag(v) for v in zd)
+    def event_at(v, t):
+        turn = 6 * (v + 1)
+        late = t - ((5 + v) * LAG - turn)
+        wrap = jnp.where(late >= turn, late, -1)
+        return jnp.where(v < 4, jnp.where((t < turn) | (v == 3), t, wrap), t - LAG * (v - 3))
+
+    def wrap4(v):
+        return jnp.where(v >= 4, v - 4, v)
 
     def source_z(d, q):
-        s = (base[d] + 4 - q) % 4
+        s = wrap4(base[d] + 4 - q)
         return s if d == 0 else 3 - s
 
     def part(zs, ys, first, rows):
@@ -245,8 +298,17 @@
     def yz_copy(d, q, j, s, ref, to):
         return remote(ref, ref, yz_send.at[d, q, j, s], yz_recv.at[d, q, j, s], to)
 
+    def x_copy(d, q, j, ref):
+        return remote(ref, ref, x_send.at[d, q, j], x_recv.at[d, q, j], twin)
+
     def yy_copy(d, s, ref, to):
         return remote(ref, ref, yy_send.at[d, s], yy_recv.at[d, s], to)
+
+    def unpack(first, last):
+        if first == 0:
+            tile_copy.wait()
+        for v in range(first, last):
+            own[v] = raw[:, v, :]
 
     def near_start():
         @pl.when(near)
@@ -254,7 +316,7 @@
             for h in range(2):
                 pltpu.make_async_copy(col0, col0, inj_recv.at[h]).wait()
             for d in range(2):
-                ref = ypart(d, z % 4, y)
+                ref = ypart(d, zown, y)
                 yy_copy(d, 0, ref, yup).start()
                 yy_copy(d, 1, ref, ydown).start()
 
@@ -262,7 +324,7 @@
         @pl.when(near)
         def _():
             for d in range(2):
-                ref = ypart(d, z % 4, yfrom[d])
+                ref = ypart(d, zown, yfrom[d])
                 yy_copy(d, d, ref, yto[d]).wait_recv()
                 yy_copy(d, 2, ref, yto[d]).start()
 
@@ -277,8 +339,8 @@
             zcopy(d, q, j, ref).start()
 
     def event(d, e):
-        q = e // 6
-        j = e % 6
+        q = jnp.where(e >= 18, 3, jnp.where(e >= 12, 2, jnp.where(e >= 6, 1, 0)))
+        j = e - 6 * q
 
         @pl.when(j < 2)
         def _():
@@ -287,11 +349,11 @@
             yz_copy(d, q, j, 0, ref, yup).start()
             yz_copy(d, q, j, 1, ref, ydown).start()
 
-        @pl.when(j >= 2)
+        @pl.when((j >= 2) & native)
         def _():
             i = j - 2
-            gray = i + i // 2 - 2 * (i // 3)
-            ref = ypart(d, source_z(d, q), (y + gray) % 4)
+            gray = jnp.where(i == 2, 3, jnp.where(i == 3, 2, i))
+            ref = ypart(d, source_z(d, q), wrap4(y + gray))
 
             for num, s in ((1, 1), (2, 0), (3, 2)):
                 if s != d:
@@ -301,6 +363,10 @@
 
             pass_on(d, q, j, ref)
 
+            @pl.when(far | (q > 0))
+            def _():
+                x_copy(d, q, i, ref).start()
+
         @pl.when((j == 3) | (j == 4))
         def _():
             ref = zpart(d, q, j - 3, yfrom[d])
@@ -310,8 +376,7 @@
     def slot(t):
         t = jnp.int32(t)
         for d in range(2):
-            late = jnp.where(t < 6, t, jnp.where(t < 10, -1, t - 4))
-            e = jnp.where(zd[d] == 0, late, t - lags[d])
+            e = event_at(zd[d], t)
 
             @pl.when((e >= 0) & (e < EVENTS))
             def _():
@@ -352,7 +417,7 @@
         def _():
             for d in range(2):
                 for s in range(3):
-                    yy_copy(d, s, ypart(d, z % 4, y), yup).wait_send()
+                    yy_copy(d, s, ypart(d, zown, y), yup).wait_send()
 
         def each(q, _):
             for d in range(2):
@@ -363,9 +428,20 @@
 
                 @pl.when(q < nsend[d])
                 def _():
-                    for j in range(6):
-                        ref = zpart(d, q, j, y) if j < 2 else ypart(d, source_z(d, q), y)
-                        zcopy(d, q, j, ref).wait_send()
+                    for j in range(2):
+                        zcopy(d, q, j, zpart(d, q, j, y)).wait_send()
+
+                @pl.when(native)
+                def _():
+                    ref = ypart(d, source_z(d, q), y)
+                    for j in range(4):
+                        @pl.when(q < nsend[d])
+                        def _():
+                            zcopy(d, q, 2 + j, ref).wait_send()
+
+                        @pl.when(far | (q > 0))
+                        def _():
+                            x_copy(d, q, j, ref).wait_send()
             return 0
 
         lax.fori_loop(0, 4, each, 0)
@@ -373,12 +449,13 @@
     near_start()
     slot(0)
     spread(0, 0, 1)
+    slot(1)
+    unpack(0, 16)
+    slot(2)
+    lead_half(0, 0, 1)
     spread(1, 1, 2)
-    slot(1)
-    lead_half(0, 0, 1)
-    slot(2)
-    lead_half(1, 1, 2)
     slot(3)
+    unpack(16, 32)
 
     eye = (
         lax.broadcasted_iota(jnp.int32, (LEAD, LEAD), 0)
@@ -395,8 +472,12 @@
         dx[:, NB : 2 * NB] = eye[0:NB, 0:NB]
 
         def between(p):
-            if p % 3 == 0 and p < 15:
-                slot(FIRST + 5 * k + p // 3)
+            if p % 3 == 0 and p < 18:
+                slot(FIRST + 6 * k + p // 3)
+            if p == 8:
+                @pl.when(k == 0)
+                def _():
+                    lead_half(1, 1, 2)
 
         diag_factor(dx, between)
 
@@ -406,13 +487,14 @@
             m[0:BS, BS:LEAD] = abuf[1].reshape(BS, BS)
             m[BS:LEAD, BS:LEAD] = abuf[2].reshape(BS, BS)
 
-        mk = dotf(dx[:, NB : 2 * NB], m[pl.ds(off, NB), :], 1, 0)
-        m[pl.ds(off, NB), :] = mk
+        span = pl.ds(off, LEAD + NB)
+        mk = dotf(dx[:, NB : 2 * NB], m[pl.ds(off, NB), span], 1, 0)
+        m[pl.ds(off, NB), span] = mk
 
         def trail(i, _):
             oi = pl.multiple_of(i * NB, NB)
             u = m[pl.ds(off, NB), pl.ds(oi, NB)]
-            m[pl.ds(oi, NB), :] = m[pl.ds(oi, NB), :] - dotf(u, mk, 0, 0)
+            m[pl.ds(oi, NB), span] = m[pl.ds(oi, NB), span] - dotf(u, mk, 0, 0)
             return 0
 
         lax.fori_loop(k + 1, LEAD // NB, trail, 0)
@@ -420,14 +502,14 @@
 
     lax.fori_loop(0, LEAD // NB, step, 0)
 
-    slot(FIRST + 20)
+    slot(28)
     w_copy.wait_recv()
     w_local.wait()
     p0 = dotf(w[0], m[0:BS, LEAD : LEAD + BS], 1, 1)
     p1 = dotf(w[0], m[BS:LEAD, LEAD : LEAD + BS], 1, 1) + dotf(w[1], m[BS:LEAD, LEAD + BS :], 1, 1)
     q_out[:, 0:BS] = dotf(p0, m[0:BS, LEAD : LEAD + BS], 1, 0) + dotf(p1, m[BS:LEAD, LEAD : LEAD + BS], 1, 0)
     q_out[:, BS:LEAD] = dotf(p1, m[BS:LEAD, LEAD + BS :], 1, 0)
-    slot(FIRST + 21)
+    slot(29)
     p_out[...] = jnp.where(core == 0, p0, p1)
     ri = lax.broadcasted_iota(jnp.int32, (BS, BS), 0)
     ci = lax.broadcasted_iota(jnp.int32, (BS, BS), 1)
@@ -448,7 +530,6 @@
     def _():
         p_out[...] = jnp.where(ri >= ci, m[BS:LEAD, BS:LEAD].T, 0.0)
 
-    tile_copy.wait()
     flat = out.reshape(BS * 32, NB)
 
     def work(i, _):
@@ -461,6 +542,21 @@
                     for s in range(3):
                         if s != d:
                             yz_copy(d, q, j, s, zpart(d, q, j, y), yup).wait_recv()
+
+            @pl.when(jnp.logical_not(native))
+            def _():
+                for d in range(2):
+                    for j in range(4):
+                        ref = ypart(d, source_z(d, q), y)
+
+                        @pl.when(far | (q > 0))
+                        def _():
+                            x_copy(d, q, j, ref).wait_recv()
+
+                    for s in YWAIT[d]:
+                        @pl.when(near & (q == 0))
+                        def _():
+                            yy_copy(d, s, ypart(d, zown, y), yup).wait_recv()
 
         for d in range(2):
             ids = [(source_z(d, q) * 4 + 2 * (i % 2) + h) * 2 + d for h in range(2)]
@@ -468,15 +564,24 @@
             upd = dotf(q_out[...], jnp.concatenate(rows, axis=0), 1, 1)
             for h in range(2):
                 where = pl.ds(ids[h], BS, stride=32)
-                flat[where, :] = flat[where, :] - upd[:, h * NB : (h + 1) * NB]
+                flat[where, :] = own[ids[h]] - upd[:, h * NB : (h + 1) * NB]
         return 0
 
-    def slot_and_work(i, _):
-        slot(FIRST + 22 + i)
-        return work(i, 0)
-
-    lax.fori_loop(0, 6, slot_and_work, 0)
-    lax.fori_loop(6, 8, work, 0)
+    def slots(first, last):
+        lax.fori_loop(first, last, lambda t, _: (slot(t), 0)[1], 0)
+
+    slots(30, 31)
+    lax.fori_loop(0, 1, work, 0)
+    slots(31, 32)
+    lax.fori_loop(1, 2, work, 0)
+    slots(32, 33)
+    lax.fori_loop(2, 3, work, 0)
+    slots(33, 34)
+    lax.fori_loop(3, 4, work, 0)
+    slots(34, 35)
+    lax.fori_loop(4, 5, work, 0)
+    slots(35, 36)
+    lax.fori_loop(5, 8, work, 0)
 
     @pl.when(xlo == 0)
     def _():
@@ -502,9 +607,11 @@
             pltpu.VMEM((3, 8, 2, PIECE, BS), jnp.float32),
             pltpu.VMEM((LEAD, 2 * LEAD), jnp.float32),
             pltpu.VMEM((NB, 2 * NB), jnp.float32),
+            pltpu.VMEM((BS, 32, NB), jnp.float32),
+            pltpu.VMEM((32, BS, NB), jnp.float32),
             dma((1,)), dma((2,)), dma((1,)), dma((1,)),
             dma((1,)), dma((3,)), dma((2,)), dma((2,)), dma((2,)), dma((2,)),
-            dma((2, 4, 6)), dma((2, 4, 6)), dma((2, 4, 2, 3)), dma((2, 4, 2, 3)), dma((2, 3)), dma((2, 3)),
+            dma((2, 4, 6)), dma((2, 4, 6)), dma((2, 4, 2, 3)), dma((2, 4, 2, 3)), dma((2, 3)), dma((2, 3)), dma((2, 4, 4)), dma((2, 4, 4)),
             dma((2,)),
         ],
         compiler_params=pltpu.CompilerParams(

time: 121 us -> 110 us (0.909)
  Pallas kernels: 117 us -> 106 us
    pallas_call x1, Pallas kernels: 117 us -> 106 us  [factor_and_update(): pl.pallas_call(gather_kernel, out_shape=jax.ShapeDtypeStruct((BS, 32, NB)...]
where the time goes in v4:
time: 110 us
  Pallas kernels  106 us (96%)
  local copies, waits for them, and re-layouts  3.33 us (3%)
    pallas_call x1, Pallas kernels, factor_and_update(): pl.pallas_call(gather_kernel, out_shape=jax.ShapeDtypeStruct((BS, 32, NB)...  106 us

profile of v4, /device:TPU:6, one launch (start us, length us, event | category | flops | bytes accessed | tf_op | source)
XLA Modules:
  0.0 109.6 jit_solution(13836168947469459585)
XLA Ops:
  0.0 1.3 %slice.4 = f32[256,2,128]{2,1,0:T(2,128)S(1)} slice(f32[256,64,128]{2,1,0:T(8,128)} %bitcast.8), slice={[0:256], [0:2], [0:128]} | slice | bytes 524288 | tf_op jit(solution)/shard_map/slice | solution.py:628
  1.3 106.3 %shard_map.17 = f32[256,32,128]{2,1,0:T(8,128)S(1)} custom-call(f32[256,256]{1,0:T(8,128)S(1)} %bitcast.7, f32[256,64,128]{2,1,0:T(8,128)} %bitcast.9), custom_call_target="tpu_custom_call" | custom-call | flops 1073741824 | bytes 16777216 | tf_op jit(solution)/shard_map/pallas_call | solution.py:597
  107.6 2.0 %copy.7 = f32[1,1,256,16,1,256]{5,4,3,2,1,0:T(1,128)} copy(f32[1,1,256,16,1,256]{5,4,3,2,1,0:T(1,128)S(1)} %bitcast.6) | data formatting | bytes 8388608
  (1 shorter events, 0.0 us)

commit v5 on v4

--- a/solution.py
+++ b/solution.py
@@ -446,16 +446,15 @@
 
         lax.fori_loop(0, 4, each, 0)
 
+    spread(0, 0, 1)
     near_start()
     slot(0)
-    spread(0, 0, 1)
     slot(1)
-    unpack(0, 16)
+    lead_half(0, 0, 1)
     slot(2)
-    lead_half(0, 0, 1)
     spread(1, 1, 2)
+    unpack(0, 32)
     slot(3)
-    unpack(16, 32)
 
     eye = (
         lax.broadcasted_iota(jnp.int32, (LEAD, LEAD), 0)

time: 110 us -> 107 us (0.973)
  Pallas kernels: 106 us -> 104 us
    pallas_call x1, Pallas kernels: 106 us -> 104 us  [factor_and_update(): pl.pallas_call(gather_kernel, out_shape=jax.ShapeDtypeStruct((BS, 32, NB)...]
where the time goes in v5:
time: 107 us
  Pallas kernels  104 us (97%)
  local copies, waits for them, and re-layouts  3.33 us (3%)
    pallas_call x1, Pallas kernels, factor_and_update(): pl.pallas_call(gather_kernel, out_shape=jax.ShapeDtypeStruct((BS, 32, NB)...  104 us

profile of v5, /device:TPU:6, one launch (start us, length us, event | category | flops | bytes accessed | tf_op | source)
XLA Modules:
  0.0 107.0 jit_solution(7491659850891341795)
XLA Ops:
  0.0 1.3 %slice.4 = f32[256,2,128]{2,1,0:T(2,128)S(1)} slice(f32[256,64,128]{2,1,0:T(8,128)} %bitcast.8), slice={[0:256], [0:2], [0:128]} | slice | bytes 524288 | tf_op jit(solution)/shard_map/slice | solution.py:627
  1.3 103.7 %shard_map.17 = f32[256,32,128]{2,1,0:T(8,128)S(1)} custom-call(f32[256,256]{1,0:T(8,128)S(1)} %bitcast.7, f32[256,64,128]{2,1,0:T(8,128)} %bitcast.9), custom_call_target="tpu_custom_call" | custom-call | flops 1073741824 | bytes 16777216 | tf_op jit(solution)/shard_map/pallas_call | solution.py:596
  105.0 2.0 %copy.7 = f32[1,1,256,16,1,256]{5,4,3,2,1,0:T(1,128)} copy(f32[1,1,256,16,1,256]{5,4,3,2,1,0:T(1,128)S(1)} %bitcast.6) | data formatting | bytes 8388608
  (1 shorter events, 0.0 us)

commit v6 on v5

--- a/solution.py
+++ b/solution.py
@@ -449,10 +449,10 @@
     spread(0, 0, 1)
     near_start()
     slot(0)
+    lead_half(0, 0, 1)
     slot(1)
-    lead_half(0, 0, 1)
+    spread(1, 1, 2)
     slot(2)
-    spread(1, 1, 2)
     unpack(0, 32)
     slot(3)
 

time: 107 us -> 107 us (level)
  no operation moved by 1% of the time
where the time goes in v6:
time: 107 us
  Pallas kernels  104 us (97%)
  local copies, waits for them, and re-layouts  3.33 us (3%)
    pallas_call x1, Pallas kernels, factor_and_update(): pl.pallas_call(gather_kernel, out_shape=jax.ShapeDtypeStruct((BS, 32, NB)...  104 us

profile of v6, /device:TPU:6, one launch (start us, length us, event | category | flops | bytes accessed | tf_op | source)
XLA Modules:
  0.0 107.3 jit_solution(8811234931073751636)
XLA Ops:
  0.0 1.3 %slice.4 = f32[256,2,128]{2,1,0:T(2,128)S(1)} slice(f32[256,64,128]{2,1,0:T(8,128)} %bitcast.8), slice={[0:256], [0:2], [0:128]} | slice | bytes 524288 | tf_op jit(solution)/shard_map/slice | solution.py:627
  1.3 104.0 %shard_map.17 = f32[256,32,128]{2,1,0:T(8,128)S(1)} custom-call(f32[256,256]{1,0:T(8,128)S(1)} %bitcast.7, f32[256,64,128]{2,1,0:T(8,128)} %bitcast.9), custom_call_target="tpu_custom_call" | custom-call | flops 1073741824 | bytes 16777216 | tf_op jit(solution)/shard_map/pallas_call | solution.py:596
  105.3 2.0 %copy.7 = f32[1,1,256,16,1,256]{5,4,3,2,1,0:T(1,128)} copy(f32[1,1,256,16,1,256]{5,4,3,2,1,0:T(1,128)S(1)} %bitcast.6) | data formatting | bytes 8388608
  (1 shorter events, 0.0 us)
